TPU v7x, 32 devices: a whole 2x2x4 slice. The times are simulated.
32 devices in a mesh: row: 4 (over y, x), col: 4 (over z), rep: 2 (over core).
Axes of the slice: x: 2, y: 2, z: 4, core: 2. Of those that a mesh axis runs over, the one named last changes fastest.
Arguments:
- amplitudes: bfloat16 [16, 16, 6, 5184], P('row', 'col', 'rep'), may hold values from -6 to 6
- integrals: bfloat16 [5184, 6, 5184], P('col', 'rep', 'row'), may hold values from -0.03125 to 0.03125
- occ_offsets: int32 [9], replicated, may hold values from 0 to 16, as said below
- slab: int32 [2], replicated, may hold values from 0 to 7
Outputs:
- residual: bfloat16 [16, 16, 5184], P('row', 'col')
Inputs may be any that keep to these rules, and one draw needn't show every extreme that they name: `occ_offsets`: never falling; entry 0 is 0 and entry 8 is 16; entries k and k+1 bound the occupied orbitals of irrep k.
All inputs are finite; a program needn't handle non-finite values.
Results may differ from a plain program's by a relative error of at most 0.02.
Values may be sent and summed in bfloat16 or wider, within the bound.
A program may use at most 128 MiB of HBM per device.

v0:
```python
import jax
import jax.numpy as jnp
from jax import lax
from jax.sharding import PartitionSpec as P


def irrep_labels(orbitals, occ_offsets):
    return jnp.sum((orbitals[:, None] >= occ_offsets[None, 1:8]).astype(jnp.int32), axis=1)


def shards(amplitudes, integrals, occ_offsets, slab):
    block_rows = amplitudes.shape[0]
    shuffled = lax.all_to_all(amplitudes, "row", split_axis=3, concat_axis=0, tiled=True)
    slab_rows = lax.all_gather(integrals, "col", axis=0, tiled=True)
    summed = lax.psum_scatter(
        jnp.einsum("ijkc,akc->ija", shuffled, slab_rows, preferred_element_type=jnp.float32).astype(
            jnp.bfloat16
        ),
        ("row", "rep"),
        scatter_dimension=0,
        tiled=True,
    )
    ladder = lax.all_gather(summed, "rep", axis=0, tiled=True)
    sectioned = lax.all_to_all(
        lax.all_to_all(ladder[None], "row", split_axis=3, concat_axis=0, tiled=True),
        "col",
        split_axis=0,
        concat_axis=0,
        tiled=True,
    )
    mirrored = lax.all_to_all(sectioned, "row", split_axis=0, concat_axis=3, tiled=True)
    mirror = jnp.swapaxes(mirrored[0], 0, 1)
    local_range = jnp.arange(block_rows, dtype=jnp.int32)
    row_orbitals = lax.axis_index("row") * block_rows + local_range
    col_orbitals = lax.axis_index("col") * block_rows + local_range
    target = jnp.bitwise_xor(slab[0], slab[1])
    row_labels = irrep_labels(row_orbitals, occ_offsets)
    col_labels = irrep_labels(col_orbitals, occ_offsets)
    allowed = jnp.bitwise_xor(row_labels[:, None], col_labels[None, :]) == target
    mixed = ladder.astype(jnp.float32) - mirror.astype(jnp.float32)
    return jnp.where(allowed[:, :, None], mixed, jnp.float32(0.0)).astype(jnp.bfloat16)


def solution(mesh):
    placed = (P("row", "col", "rep", None), P("col", "rep", "row"), P(), P())
    return jax.shard_map(
        shards, mesh=mesh, in_specs=placed, out_specs=P("row", "col", None), check_vma=False
    )
```

profile of v0, /device:TPU:1, one launch (start us, length us, event | category | flops | bytes accessed | tf_op | source)
XLA Modules:
  0.0 887.0 jit_solution(79836557311175437)
XLA Ops:
  6.5 0.7 all-gather.2.cloned.1.call-update
  7.3 19.0 %copy.20 = bf16[4,4,3,5184]{1,0,2,3:T(4,128)(2,1)} copy(bf16[4,4,3,5184]{3,1,2,0:T(4,128)(2,1)} %param.4) | data formatting | bytes 995328 | tf_op args[0]
  26.3 36.2 %reshape.48 = bf16[4,2,31104]{2,1,0:T(2,128)(2,1)S(1)} reshape(bf16[5184,3,4,4]{3,2,1,0:T(4,128)(2,1)} %bitcast.42) | data formatting | bytes 995328
  62.5 11.2 %all_to_all.50 = bf16[4,2,31104]{2,1,0:T(2,128)(2,1)S(1)} all-to-all(bf16[4,2,31104]{2,1,0:T(2,128)(2,1)S(1)} %reshape.48), channel_id=1, replica_groups=mesh['row'=4,'col'=4,'rep'=2] {'row'}, dimensions={0} | all-to-all | bytes 995328 | tf_op jit(solution)/shard_map/all_to_all | solution.py:13
  73.7 38.2 %reshape.49 = bf16[5184,3,4,4]{3,2,1,0:T(4,128)(2,1)} reshape(bf16[4,2,31104]{2,1,0:T(2,128)(2,1)S(1)} %all_to_all.50) | data formatting | bytes 995328
  111.9 24.1 %copy.21 = bf16[4,4,3,4,1296]{4,0,3,2,1:T(4,128)(2,1)S(1)} copy(bf16[4,4,3,4,1296]{1,0,2,4,3:T(4,128)(2,1)} %bitcast.41) | data formatting | bytes 995328 | tf_op jit(solution)/shard_map/all_to_all | solution.py:13
  136.3 604.0 %all-gather.2.cloned.1.call-done = bf16[5184,3,1296]{2,0,1:T(8,128)(2,1)} async-done(((bf16[1296,3,1296]{2,0,1:T(8,128)(2,1)}), bf16[5184,3,1296]{2,0,1:T(8,128)(2,1)}) %all-gather.2.cloned.1.call-update) | async-done | bytes 40310800 | tf_op jit(solution)/shard_map/all_gather | solution.py:14
  740.3 19.2 %fusion.5 = bf16[16,4,5184]{2,0,1:T(8,128)(2,1)S(1)} fusion(bf16[16,4,3,1296]{3,0,2,1:T(8,128)(2,1)S(1)} %all_to_all.39, bf16[5184,3,1296]{2,0,1:T(8,128)(2,1)} %all-gather.2.cloned.1.call-done), kind=kOutput, calls=%fused_computation.3 | convolution fusion | flops 2580221952 | bytes 41472000 | tf_op jit(solution)/shard_map/ijkc,akc->ija/dot_general | solution.py:16
  759.5 1.1 copy.22
  760.7 0.6 dynamic-slice
  761.9 51.2 %all-reduce.3.cloned.1.call-done = bf16[16,4,5184]{2,1,0:T(4,128)(2,1)} async-done(((bf16[16,4,5184]{2,1,0:T(4,128)(2,1)}), bf16[16,4,5184]{2,1,0:T(4,128)(2,1)}) %all-reduce.3.cloned.1.call-update) | async-done | bytes 663568
  813.2 0.9 constant_dynamic-slice_fusion
  814.1 2.5 all_gather.7
  816.6 5.8 copy.23
  822.4 11.1 %reshape.50 = bf16[4,2,10368]{2,1,0:T(2,128)(2,1)S(1)} reshape(bf16[5184,1,4,4]{3,2,1,0:T(4,128)(2,1)} %bitcast.44) | data formatting | bytes 331776
  833.5 6.8 all_to_all.51
  840.3 12.8 %reshape.51 = bf16[5184,1,4,4]{3,2,1,0:T(4,128)(2,1)} reshape(bf16[4,2,10368]{2,1,0:T(2,128)(2,1)S(1)} %all_to_all.51) | data formatting | bytes 331776
  853.1 9.0 %copy.24 = bf16[1,4,4,4,1296]{4,1,2,3,0:T(4,128)(2,1)} copy(bf16[1,4,4,4,1296]{1,2,4,3,0:T(4,128)(2,1)} %bitcast.43) | data formatting | bytes 331776 | tf_op jit(solution)/shard_map/all_to_all | solution.py:25
  862.1 4.3 all-to-all-start.2
  866.5 0.6 fusion.10
  868.7 2.8 all-to-all-done.2
  871.5 3.4 all-to-all-start.3
  875.0 3.9 all-to-all-done.3
  879.4 0.8 fusion.9
  (17 shorter events, 1.2 us)
Async XLA Ops:
  6.5 733.8 %all-gather.2.cloned.1.call-start = ((), (), s32[]{:S(2)}) async-start(), calls=%async_computation.4 | async-start | bytes 54743040 | tf_op jit(solution)/shard_map/all_gather | solution.py:14
  7.3 805.9 %all-reduce.3.cloned.1.call-start = ((), (), s32[]{:S(2)}) async-start(), calls=%async_computation.5 | async-start | bytes 1343488
  136.3 624.4 %copy-start.2 = (u32[32]{0:T(128)S(1)}, u32[32]{0:T(128)}, u32[]{:S(2)}) copy-start(u32[32]{0:T(128)} %constant.19) | copy-start | bytes 388
  759.5 106.9 %copy-start = (s32[2]{0:T(128)S(1)}, s32[2]{0:T(128)}, u32[]{:S(2)}) copy-start(s32[2]{0:T(128)} %param.7) | copy-start | bytes 28
  759.5 107.5 %copy-start.1 = (s32[9]{0:T(128)S(1)}, s32[9]{0:T(128)}, u32[]{:S(2)}) copy-start(s32[9]{0:T(128)} %param.6) | copy-start | bytes 112
  862.1 9.4 %all-to-all-start.2 = ((bf16[4,4,4,1296]{3,1,2,0:T(4,128)(2,1)}), bf16[4,4,4,1296]{3,1,2,0:T(4,128)(2,1)}, u32[]{:S(2)}, u32[]{:S(2)}) async-start(bf16[4,4,4,1296]{3,1,2,0:T(4,128)(2,1)} %bitcast.9), calls=%async_computation.2 | async-start | bytes 360448 | tf_op jit(solution)/shard_map/all_to_all | solution.py:24
  871.5 7.3 all-to-all-start.3
Sparse Core Ops, SparseCore 0:
  8.9 731.3 all-gather.1
  760.8 52.3 all-reduce.2
where the time goes:
time: 894 us; the launch traced here: 887 us
  waiting for transfers between devices  663 us (74%)
  local copies, waits for them, and re-layouts  160 us (18%)
  blocking collectives  20.5 us (2%)
  matrix products  19.2 us (2%)
  between operations  15.5 us (2%)
    all_gather x1, waiting for transfers between devices, shards(): slab_rows = lax.all_gather(integrals, 'col', axis=0, tiled=True)  604 us
    unnamed x13, local copies, waits for them, and re-layouts  119 us
    unnamed x3, waiting for transfers between devices  52 us
    all_to_all x2, local copies, waits for them, and re-layouts, shards(): lax.all_to_all(amplitudes, 'row', split_axis=3, concat_axis=0, tiled=True)  24.3 us
    dot_general x1, matrix products, shards(): jnp.einsum('ijkc,akc->ija', shuffled, slab_rows, preferred_element_type=j...  19.2 us
  transfers between devices with their start and end apart: 4, of which 4 were waited for; matrix products, arithmetic and copies ran while one was open for 13% of the time, Pallas kernels for 0%

commit v1 on v0

v1 whole, which is shorter than its diff:
```python
import jax
import jax.numpy as jnp
from jax import lax
from jax.sharding import PartitionSpec as P


def irrep_labels(orbitals, occ_offsets):
    return jnp.sum((orbitals[:, None] >= occ_offsets[None, 1:8]).astype(jnp.int32), axis=1)


def shards(amplitudes, integrals, occ_offsets, slab):
    block_rows, block_cols = amplitudes.shape[:2]
    shuffled = lax.all_to_all(amplitudes, "row", split_axis=3, concat_axis=0, tiled=True)
    amps = lax.all_gather(shuffled, "col", axis=1, tiled=True)
    partial = jnp.einsum("ijkc,akc->ija", amps, integrals, preferred_element_type=jnp.float32)
    mixed = (partial - jnp.swapaxes(partial, 0, 1)).astype(jnp.bfloat16)
    summed = lax.psum_scatter(mixed, ("row", "rep"), scatter_dimension=0, tiled=True)
    summed = lax.all_to_all(summed, "col", split_axis=1, concat_axis=2, tiled=True)
    ladder = lax.all_gather(summed, "rep", axis=0, tiled=True)
    row_orbitals = lax.axis_index("row") * block_rows + jnp.arange(block_rows, dtype=jnp.int32)
    col_orbitals = lax.axis_index("col") * block_cols + jnp.arange(block_cols, dtype=jnp.int32)
    target = jnp.bitwise_xor(slab[0], slab[1])
    row_labels = irrep_labels(row_orbitals, occ_offsets)
    col_labels = irrep_labels(col_orbitals, occ_offsets)
    allowed = jnp.bitwise_xor(row_labels[:, None], col_labels[None, :]) == target
    return jnp.where(allowed[:, :, None], ladder, jnp.bfloat16(0.0))


def solution(mesh):
    placed = (P("row", "col", "rep", None), P("col", "rep", "row"), P(), P())
    return jax.shard_map(
        shards, mesh=mesh, in_specs=placed, out_specs=P("row", "col", None), check_vma=False
    )
```

time: 894 us -> 252 us (0.28)
  waiting for transfers between devices: 663 us -> 84.3 us
  local copies, waits for them, and re-layouts: 160 us -> 120 us
  matrix products: 19.2 us -> 8.39 us
    all_gather x1, waiting for transfers between devices: 604 us -> 48.5 us  [shards(): amps = lax.all_gather(shuffled, 'col', axis=1, tiled=True)]
    unnamed x3 -> x2, waiting for transfers between devices: 52 us -> 0.03 us
    reduce_scatter x0 -> x1, waiting for transfers between devices: none -> 31.1 us  [shards(): lax.psum_scatter(mixed, ('row', 'rep'), scatter_dimension=0, tiled=True)]
    unnamed x13 -> x7, local copies, waits for them, and re-layouts: 119 us -> 92.3 us
    dot_general x1, matrix products: 19.2 us -> 8.39 us  [shards(): jnp.einsum('ijkc,akc->ija', amps, integrals, preferred_element_type=jnp.f...]
  transfers between devices with their start and end apart: 4 -> 3, of which waited for: 4 -> 3; matrix products, arithmetic and copies ran while one was open for 13% -> 0% of each run, Pallas kernels for 0% -> 0%
where the time goes in v1:
time: 252 us; the launch traced here: 249 us
  local copies, waits for them, and re-layouts  120 us (48%)
  waiting for transfers between devices  84.3 us (33%)
  blocking collectives  15.1 us (6%)
  between operations  14.7 us (6%)
  matrix products  8.39 us (3%)
  starting transfers between devices  4.35 us (2%)
    unnamed x7, local copies, waits for them, and re-layouts  92.3 us
    all_gather x1, waiting for transfers between devices, shards(): amps = lax.all_gather(shuffled, 'col', axis=1, tiled=True)  48.5 us
    reduce_scatter x1, waiting for transfers between devices, shards(): lax.psum_scatter(mixed, ('row', 'rep'), scatter_dimension=0, tiled=True)  31.1 us
    all_to_all x2, local copies, waits for them, and re-layouts, shards(): lax.all_to_all(amplitudes, 'row', split_axis=3, concat_axis=0, tiled=True)  25.1 us
    all_to_all x1, blocking collectives, shards(): lax.all_to_all(amplitudes, 'row', split_axis=3, concat_axis=0, tiled=True)  11.2 us
    dot_general x1, matrix products, shards(): jnp.einsum('ijkc,akc->ija', amps, integrals, preferred_element_type=jnp.f...  8.39 us
  transfers between devices with their start and end apart: 3, of which 3 were waited for; matrix products, arithmetic and copies ran while one was open for 0% of the time, Pallas kernels for 0%

profile of v1, /device:TPU:1, one launch (start us, length us, event | category | flops | bytes accessed | tf_op | source)
XLA Modules:
  0.0 249.1 jit_solution(3933676895512804169)
XLA Ops:
  6.5 18.9 %copy.20 = bf16[4,4,3,5184]{1,0,2,3:T(4,128)(2,1)} copy(bf16[4,4,3,5184]{3,1,2,0:T(4,128)(2,1)} %param.4) | data formatting | bytes 995328 | tf_op args[0]
  25.5 35.1 %reshape.40 = bf16[4,2,31104]{2,1,0:T(2,128)(2,1)S(1)} reshape(bf16[5184,3,4,4]{3,2,1,0:T(4,128)(2,1)} %bitcast.24) | data formatting | bytes 995328
  60.6 11.2 %all_to_all.36 = bf16[4,2,31104]{2,1,0:T(2,128)(2,1)S(1)} all-to-all(bf16[4,2,31104]{2,1,0:T(2,128)(2,1)S(1)} %reshape.40), channel_id=1, replica_groups=mesh['row'=4,'col'=4,'rep'=2] {'row'}, dimensions={0} | all-to-all | bytes 995328 | tf_op jit(solution)/shard_map/all_to_all | solution.py:13
  71.8 38.2 %reshape.41 = bf16[5184,3,4,4]{3,2,1,0:T(4,128)(2,1)} reshape(bf16[4,2,31104]{2,1,0:T(2,128)(2,1)S(1)} %all_to_all.36) | data formatting | bytes 995328
  110.0 24.0 %copy.21 = bf16[4,4,4,3,1296]{4,1,0,3,2:T(4,128)(2,1)S(1)} copy(bf16[4,4,4,3,1296]{2,1,3,4,0:T(4,128)(2,1)} %bitcast.23) | data formatting | bytes 995328 | tf_op jit(solution)/shard_map/all_to_all | solution.py:13
  134.0 1.1 all_to_all.29
  135.1 0.0 all-gather.2.cloned.1.call-update
  135.1 0.0 reduce-scatter.2.cloned.1.call-start
  135.2 48.5 %all-gather.2.cloned.1.call-done = bf16[16,16,3,1296]{3,0,2,1:T(8,128)(2,1)} async-done(((bf16[16,4,3,1296]{3,0,2,1:T(8,128)(2,1)}), bf16[16,16,3,1296]{3,0,2,1:T(8,128)(2,1)}) %all-gather.2.cloned.1.call-update) | async-done | bytes 1990672 | tf_op jit(solution)/shard_map/all_gather | solution.py:14
  183.7 8.4 %fusion.2 = f32[16,16,1296]{2,1,0:T(8,128)S(1)} fusion(bf16[1296,3,1296]{2,0,1:T(8,128)(2,1)} %param.5, bf16[16,16,3,1296]{3,0,2,1:T(8,128)(2,1)} %all-gather.2.cloned.1.call-done), kind=kOutput, calls=%fused_computation.2 | convolution fusion | flops 2579890176 | bytes 13395456 | tf_op jit(solution)/shard_map/ijkc,akc->ija/dot_general | solution.py:15
  192.1 0.0 copy-start.1
  192.1 1.3 fusion.6
  193.4 0.0 reduce-scatter.2.cloned.1.call-update
  193.4 0.1 slice.10
  193.5 0.6 fusion.7
  195.4 0.2 convert_reduce_fusion.1
  195.6 31.1 %reduce-scatter.2.cloned.1.call-done = bf16[2,16,1296]{2,1,0:T(8,128)(2,1)} async-done(((bf16[16,16,1296]{2,1,0:T(8,128)(2,1)}), bf16[2,16,1296]{2,1,0:T(8,128)(2,1)}) %reduce-scatter.2.cloned.1.call-update) | async-done | bytes 82960 | tf_op jit(solution)/shard_map/reduce_scatter | solution.py:17
  226.7 1.6 copy.24
  228.3 4.3 %all-to-all-start.1 = ((bf16[2,16,1296]{2,0,1:T(2,128)(2,1)}), bf16[2,16,1296]{2,0,1:T(2,128)(2,1)S(1)}, u32[]{:S(2)}, u32[]{:S(2)}) async-start(bf16[2,16,1296]{2,0,1:T(2,128)(2,1)} %copy.24), calls=%async_computation.2 | async-start | bytes 180224 | tf_op jit(solution)/shard_map/all_to_all | solution.py:18
  232.6 0.1 xor_compare_fusion
  232.7 4.7 %all-to-all-done.1 = bf16[2,16,1296]{2,0,1:T(2,128)(2,1)S(1)} async-done(((bf16[2,16,1296]{2,0,1:T(2,128)(2,1)}), bf16[2,16,1296]{2,0,1:T(2,128)(2,1)S(1)}, u32[]{:S(2)}, u32[]{:S(2)}) %all-to-all-start.1) | async-done | bytes 82976 | tf_op jit(solution)/shard_map/all_to_all | solution.py:18
  237.4 0.1 all_to_all.33
  237.5 3.9 %all_gather.7 = bf16[4,4,5184]{2,1,0:T(4,128)(2,1)S(1)} all-gather(bf16[2,4,5184]{2,1,0:T(4,128)(2,1)S(1)} %all_to_all.33), channel_id=1, replica_groups=mesh['row'=4,'col'=4,'rep'=2] {'rep'}, dimensions={0}, use_global_device_ids=true | all-gather | bytes 248832 | tf_op jit(solution)/shard_map/all_gather | solution.py:19
  241.5 0.8 broadcast_select_fusion
  (6 shorter events, 0.1 us)
Async XLA Ops:
  6.5 177.1 %all-gather.2.cloned.1.call-start = ((), (), s32[]{:S(2)}) async-start(), calls=%async_computation.3 | async-start | bytes 2703360 | tf_op jit(solution)/shard_map/all_gather | solution.py:14
  135.1 91.5 %reduce-scatter.2.cloned.1.call-start = ((), (), s32[]{:S(2)}) async-start(), calls=%async_computation.4 | async-start | bytes 811008 | tf_op jit(solution)/shard_map/reduce_scatter | solution.py:17
  192.1 1.4 copy-start.1
  192.1 1.4 copy-start
  228.3 9.1 %all-to-all-start.1 = ((bf16[2,16,1296]{2,0,1:T(2,128)(2,1)}), bf16[2,16,1296]{2,0,1:T(2,128)(2,1)S(1)}, u32[]{:S(2)}, u32[]{:S(2)}) async-start(bf16[2,16,1296]{2,0,1:T(2,128)(2,1)} %copy.24), calls=%async_computation.2 | async-start | bytes 180224 | tf_op jit(solution)/shard_map/all_to_all | solution.py:18
Sparse Core Ops, SparseCore 0:
  135.3 48.3 all-gather.1
  193.5 33.1 reduce-scatter.1

commit v2 on v1

v2 whole, which is shorter than its diff:
```python
import functools

import jax
import jax.numpy as jnp
from jax import lax
from jax.experimental import pallas as pl
from jax.experimental.pallas import tpu as pltpu
from jax.sharding import PartitionSpec as P

MESH = pl.DeviceIdType.MESH


def irrep_labels(orbitals, occ_offsets):
    return jnp.sum((orbitals[:, None] >= occ_offsets[None, 1:8]).astype(jnp.int32), axis=1)


def pair_start(first, n):
    return first * n - first * (first - 1) // 2


def kernel(n, reps, s_ref, v_hbm, out_ref, x, dd, v, acc, pb, rrecv, qb, rowrecv, res,
           lv, a_send, a_recv, l_send, r_send, x_recv, p_send, p_recv, q_send, q_recv,
           o_send, o_recv):
    kb = s_ref.shape[1]
    per_rep = pb.shape[1]
    slots = res.shape[0]
    r, z, p = lax.axis_index("row"), lax.axis_index("col"), lax.axis_index("rep")

    def remote(src, dst, send, recv, **where):
        target = {"row": r, "col": z, "rep": p, **where}
        return pltpu.make_async_remote_copy(
            src_ref=src, dst_ref=dst, send_sem=send, recv_sem=recv,
            device_id=(target["row"], target["col"], target["rep"]), device_id_type=MESH)

    for k in range(kb):
        pltpu.make_async_copy(v_hbm.at[k], v.at[k], lv.at[k]).start()

    barrier = pltpu.get_barrier_semaphore()
    devices = n * n * reps
    me = (r * n + z) * reps + p

    @pl.loop(1, devices)
    def _(off):
        other = lax.rem(me + off, devices)
        pl.semaphore_signal(
            barrier, inc=1,
            device_id=(other // (n * reps), lax.rem(other // reps, n), lax.rem(other, reps)),
            device_id_type=MESH)

    pl.semaphore_wait(barrier, devices - 1)

    def shuffle(k, off):
        dest = lax.rem(r + off, n)
        return remote(s_ref.at[dest, k], x.at[k, z, r], a_send.at[k, off - 1],
                      a_recv.at[k, off - 1], row=dest)

    def shuffled(k, off):
        source = lax.rem(r + n - off, n)
        return remote(s_ref.at[source, k], x.at[k, z, source], a_send.at[k, off - 1],
                      a_recv.at[k, off - 1], row=source)

    for k in range(kb):
        for off in range(1, n):
            shuffle(k, off).start()
        x[k, z, r] = s_ref[r, k]
    acc[...] = jnp.zeros_like(acc)
    if reps * per_rep != n * (n + 1) // 2:
        dd[...] = jnp.zeros_like(dd)

    def to_left(k, c):
        part = x.at[k, c, pl.ds(0, c + 1)]
        return remote(part, part, l_send.at[k, c], x_recv.at[k, c], col=lax.max(z - 1, 0))

    def to_right(k, c):
        part = x.at[k, c, pl.ds(c, n - c)]
        return remote(part, part, r_send.at[k, c], x_recv.at[k, c], col=lax.min(z + 1, n - 1))

    for k in range(kb):
        for off in range(1, n):
            shuffled(k, off).wait_recv()
        for c in range(n):
            @pl.when(z == c)
            def _():
                if c > 0:
                    to_left(k, c).start()
                if c < n - 1:
                    to_right(k, c).start()

    def assemble(k, first, second):
        number = pair_start(first, n) + second - first
        slot = lax.rem(number, reps) * per_rep + number // reps

        @pl.when(z <= first)
        def _():
            dd[slot] = x[k, second, first]

        @pl.when((z >= second) & (z > first))
        def _():
            dd[slot] = x[k, first, second]

        @pl.when((z > first) & (z < second))
        def _():
            dd[slot] = (x[k, second, first].astype(jnp.float32)
                        - x[k, first, second].astype(jnp.float32)).astype(dd.dtype)

    def arrivals(k, d):
        for c in range(n):
            if c >= d:
                @pl.when(z == c - d)
                def _():
                    to_left(k, c).wait_recv()
                    x[k, c, c - d] = (x[k, c, c - d].astype(jnp.float32)
                                      - x[k, c - d, c].astype(jnp.float32)).astype(x.dtype)
                    if c > d:
                        to_left(k, c).start()
            if c + d < n:
                @pl.when(z == c + d)
                def _():
                    to_right(k, c).wait_recv()
                    x[k, c, c + d] = (x[k, c + d, c].astype(jnp.float32)
                                      - x[k, c, c + d].astype(jnp.float32)).astype(x.dtype)
                    if c + d < n - 1:
                        to_right(k, c).start()

    for d in range(1, n):
        @pl.loop(0, kb)
        def _(k):
            arrivals(k, d)
            if d == n - 1:
                @pl.loop(0, n)
                def _(first):
                    @pl.loop(first, n)
                    def _(second):
                        assemble(k, first, second)

                pltpu.make_async_copy(v_hbm.at[k], v.at[k], lv.at[k]).wait()
                acc[...] += lax.dot_general(
                    dd[...].reshape(acc.shape[0], dd.shape[2]), v[k],
                    (((1,), (1,)), ((), ())), preferred_element_type=jnp.float32)

    pb[...] = acc[...].reshape(pb.shape).astype(pb.dtype)

    def swap_reps(off):
        other = lax.rem(p + off, reps)
        return remote(pb.at[other], rrecv.at[off - 1], p_send.at[off - 1], p_recv.at[off - 1],
                      rep=other)

    for off in range(1, reps):
        swap_reps(off).start()
    for off in range(1, reps):
        swap_reps(off).wait_recv()

    flip = lax.rem(p, 2)

    def owner(q):
        return lax.rem(q, n) * (1 - 2 * flip) + (n - 1) * flip

    def to_owner(q):
        return remote(qb.at[q], rowrecv.at[q // n, r], q_send.at[q],
                      q_recv.at[q // n, r], row=owner(q))

    for q in range(per_rep):
        total = pb[p, q].astype(jnp.float32)
        for off in range(1, reps):
            total += rrecv[off - 1, q].astype(jnp.float32)
        qb[q] = total.astype(qb.dtype)

        @pl.when(owner(q) != r)
        def _():
            to_owner(q).start()

    mine = r * (1 - 2 * flip) + (n - 1) * flip

    def deliver(s, do):
        number = (s * n + mine) * reps + p
        first = 0
        for t in range(1, n):
            first = first + (number >= pair_start(t, n)).astype(jnp.int32)
        second = number - pair_start(first, n) + first
        for rep in range(reps):
            for t, (row, col) in enumerate(((first, second), (second, first))):
                local = (row == r) & (col == z) & (p == rep)
                wanted = (first != second) if t else (first == first)

                @pl.when(wanted & local)
                def _():
                    if do == "start":
                        pltpu.make_async_copy(res.at[s], out_ref.at[z], o_recv.at[z]).start()

                @pl.when(wanted & jnp.logical_not(local))
                def _():
                    copy = remote(res.at[s], out_ref.at[z], o_send.at[s, rep, t], o_recv.at[z],
                                  row=row, col=col, rep=rep)
                    if do == "start":
                        copy.start()
                    else:
                        copy.wait_send()

    for s in range(slots):
        @pl.when(s * n + mine < per_rep)
        def _():
            total = qb[s * n + mine].astype(jnp.float32)
            for off in range(1, n):
                source = lax.rem(r + off, n)
                remote(rowrecv.at[s, source], rowrecv.at[s, source], q_send.at[0],
                       q_recv.at[s, source], row=source).wait_recv()
                total += rowrecv[s, source].astype(jnp.float32)
            res[s] = total.astype(res.dtype)
            deliver(s, "start")

    for source in range(n):
        remote(out_ref.at[source], out_ref.at[source], o_send.at[0, 0, 0], o_recv.at[source],
               col=source).wait_recv()

    for s in range(slots):
        @pl.when(s * n + mine < per_rep)
        def _():
            deliver(s, "wait")
    for q in range(per_rep):
        @pl.when(owner(q) != r)
        def _():
            to_owner(q).wait_send()
    for off in range(1, reps):
        swap_reps(off).wait_send()

    @pl.loop(0, kb)
    def _(k):
        for off in range(1, n):
            shuffle(k, off).wait_send()
        for c in range(n):
            if c > 0:
                @pl.when((z <= c) & (z > 0))
                def _():
                    to_left(k, c).wait_send()
            if c < n - 1:
                @pl.when((z >= c) & (z < n - 1))
                def _():
                    to_right(k, c).wait_send()


def ladder_blocks(staged, integrals, n, reps):
    kb, rows, width = staged.shape[1:]
    slab_rows = integrals.shape[1]
    per_rep = -(-(n * (n + 1) // 2) // reps)
    slots = -(-per_rep // n)
    bf16, dma = jnp.bfloat16, pltpu.SemaphoreType.DMA
    return pl.pallas_call(
        functools.partial(kernel, n, reps),
        out_shape=jax.ShapeDtypeStruct((n, rows, slab_rows), bf16),
        in_specs=[pl.BlockSpec(memory_space=pltpu.VMEM), pl.BlockSpec(memory_space=pl.ANY)],
        out_specs=pl.BlockSpec(memory_space=pl.ANY),
        scratch_shapes=[
            pltpu.VMEM((kb, n, n, rows, width), bf16),
            pltpu.VMEM((reps * per_rep, rows, width), bf16),
            pltpu.VMEM((kb, slab_rows, width), bf16),
            pltpu.VMEM((reps * per_rep * rows, slab_rows), jnp.float32),
            pltpu.VMEM((reps, per_rep, rows, slab_rows), bf16),
            pltpu.VMEM((max(reps - 1, 1), per_rep, rows, slab_rows), bf16),
            pltpu.VMEM((per_rep, rows, slab_rows), bf16),
            pltpu.VMEM((slots, n, rows, slab_rows), bf16),
            pltpu.VMEM((slots, rows, slab_rows), bf16),
            dma((kb,)),
            dma((kb, n - 1)),
            dma((kb, n - 1)),
            dma((kb, n)),
            dma((kb, n)),
            dma((kb, n)),
            dma((max(reps - 1, 1),)),
            dma((max(reps - 1, 1),)),
            dma((per_rep,)),
            dma((slots, n)),
            dma((slots, reps, 2)),
            dma((n,)),
        ],
        compiler_params=pltpu.CompilerParams(
            collective_id=0, has_side_effects=True, vmem_limit_bytes=56 * 1024 * 1024),
        name="ladder_blocks",
    )(staged, integrals)


def shards(n, reps, amplitudes, integrals, occ_offsets, slab):
    block, _, kb, pairs = amplitudes.shape
    r, z = lax.axis_index("row"), lax.axis_index("col")
    natural = jnp.transpose(amplitudes.reshape(block, block, kb, n, pairs // n), (3, 2, 0, 1, 4))
    swapped = jnp.swapaxes(natural, 2, 3)
    mixed = (natural.astype(jnp.float32) - swapped.astype(jnp.float32)).astype(natural.dtype)
    staged = jnp.where(r < z, natural, jnp.where(r > z, swapped, mixed))
    staged = staged.reshape(n, kb, block * block, pairs // n)
    blocks = ladder_blocks(staged, jnp.transpose(integrals, (1, 0, 2)), n, reps)
    slab_rows = integrals.shape[0]
    found = jnp.transpose(blocks.reshape(n, block, block, slab_rows), (1, 2, 0, 3))
    found = found.reshape(block, block, n * slab_rows)
    found = jnp.where(r <= z, found, -jnp.swapaxes(found, 0, 1))
    row_orbitals = r * block + jnp.arange(block, dtype=jnp.int32)
    col_orbitals = z * block + jnp.arange(block, dtype=jnp.int32)
    target = jnp.bitwise_xor(slab[0], slab[1])
    row_labels = irrep_labels(row_orbitals, occ_offsets)
    col_labels = irrep_labels(col_orbitals, occ_offsets)
    allowed = jnp.bitwise_xor(row_labels[:, None], col_labels[None, :]) == target
    return jnp.where(allowed[:, :, None], found, jnp.bfloat16(0.0))


def solution(mesh):
    placed = (P("row", "col", "rep", None), P("col", "rep", "row"), P(), P())
    n, reps = mesh.shape["row"], mesh.shape["rep"]
    assert mesh.shape["col"] == n
    return jax.shard_map(
        functools.partial(shards, n, reps), mesh=mesh, in_specs=placed,
        out_specs=P("row", "col", None), check_vma=False
    )
```

time: 252 us -> 63.3 us (0.25)
  the two profiles are of different devices: /device:TPU:1 before, /device:TPU:0 now
where the time goes in v2:
time: 63.3 us; the launch traced here: 63.1 us
  Pallas kernels  54.1 us (85%)
  local copies, waits for them, and re-layouts  6.04 us (10%)
  other arithmetic  1.51 us (2%)
  between operations  1.39 us (2%)
    pallas_call x1, Pallas kernels, ladder_blocks(): pl.pallas_call(functools.partial(kernel, n, reps), out_shape=jax.ShapeDty...  54.1 us
    reshape x1, local copies, waits for them, and re-layouts, shards(): amplitudes.reshape(block, block, kb, n, pairs // n)  1.7 us
    slice x1, local copies, waits for them, and re-layouts, shards(): target = jnp.bitwise_xor(slab[0], slab[1])  1.33 us

profile of v2, /device:TPU:0, one launch (start us, length us, event | category | flops | bytes accessed | tf_op | source)
XLA Modules:
  0.0 63.1 jit_solution(4106463702602836439)
XLA Ops:
  0.0 0.7 %slice.10 = s32[7]{0:T(128)S(1)} slice(s32[9]{0:T(128)} %param.6), slice={[1:8]} | slice | bytes 56 | tf_op jit(solution)/shard_map/slice | solution.py:14
  0.7 0.2 convert_reduce_fusion.1
  0.9 1.3 %fusion.3 = (s32[1]{0:T(128)}, s32[1]{0:T(128)}) fusion(s32[2]{0:T(128)} %param.7), kind=kLoop, calls=%fused_computation.10 | loop fusion | bytes 16 | tf_op jit(solution)/shard_map/slice | solution.py:296
  3.6 0.1 xor_compare_fusion
  3.7 1.7 %reshape.50 = bf16[4,4,3,4,1296]{4,3,1,2,0:T(4,128)(2,1)S(1)} reshape(bf16[4,4,3,5184]{3,1,2,0:T(4,128)(2,1)} %param.4) | data formatting | bytes 995328 | tf_op jit(solution)/shard_map/reshape | solution.py:284
  5.4 0.4 fusion.1
  5.8 1.0 %reshape.51.s_ref = bf16[4,3,16,1296]{3,2,1,0:T(8,128)(2,1)} reshape(bf16[4,3,4,4,1296]{4,3,2,1,0:T(4,128)(2,1)S(1)} %fusion.1) | data formatting | bytes 995328 | tf_op jit(solution)/shard_map/reshape | solution.py:288
  6.9 54.1 %ladder_blocks.1 = bf16[4,16,1296]{2,1,0:T(8,128)(2,1)} custom-call(bf16[4,3,16,1296]{3,2,1,0:T(8,128)(2,1)} %reshape.51.s_ref, bf16[3,1296,1296]{2,1,0:T(8,128)(2,1)} %bitcast.15), custom_call_target="tpu_custom_call" | custom-call | tf_op jit(solution)/shard_map/ladder_blocks/pallas_call | solution.py:247
  61.0 1.0 %reshape.52 = bf16[4,4,4,1296]{3,2,1,0:T(4,128)(2,1)S(1)} reshape(bf16[4,16,1296]{2,1,0:T(8,128)(2,1)} %ladder_blocks.1) | data formatting | bytes 331776 | tf_op jit(solution)/shard_map/reshape | solution.py:291
  62.0 0.1 copy.11
  62.1 0.2 reshape.53
  62.3 0.8 %fusion.2 = bf16[4,4,5184]{2,1,0:T(4,128)(2,1)} fusion(bf16[4,4,5184]{2,0,1:T(4,128)(2,1)S(1)} %reshape.53, pred[]{:T(512)S(6)} %le.3, pred[4,4]{1,0:T(4,128)(4,1)S(1)} %xor_compare_fusion), kind=kLoop, calls=%fused_computation.4 | loop fusion | flops 248832 | bytes 331793 | tf_op jit(solution)/shard_map/jit(_where)/select_n | solution.py:300
  (1 shorter events, 0.0 us)

commit v3 on v2

--- a/solution.py
+++ b/solution.py
@@ -11,19 +11,47 @@
 
 
 def irrep_labels(orbitals, occ_offsets):
-    return jnp.sum((orbitals[:, None] >= occ_offsets[None, 1:8]).astype(jnp.int32), axis=1)
+    bound = jnp.arange(occ_offsets.shape[0], dtype=jnp.int32)
+    inner = (bound >= 1) & (bound < occ_offsets.shape[0] - 1)
+    return jnp.sum(((orbitals[:, None] >= occ_offsets[None, :]) & inner[None, :]).astype(jnp.int32), axis=1)
 
 
 def pair_start(first, n):
-    return first * n - first * (first - 1) // 2
-
-
-def kernel(n, reps, s_ref, v_hbm, out_ref, x, dd, v, acc, pb, rrecv, qb, rowrecv, res,
-           lv, a_send, a_recv, l_send, r_send, x_recv, p_send, p_recv, q_send, q_recv,
+    return first * (n - 1) - first * (first - 1) // 2
+
+
+def swap_rows(block, size):
+    return jnp.concatenate(
+        [block[i * size + j : i * size + j + 1] for j in range(size) for i in range(size)], axis=0)
+
+
+def pack_rows(block, size):
+    above = [block[i * size + i + 1 : (i + 1) * size] for i in range(size - 1)]
+    rest = size * size // 2 - size * (size - 1) // 2
+    return jnp.concatenate(above + [jnp.zeros_like(block[:rest])], axis=0)
+
+
+def unpack_rows(packed, size):
+    rows, at = {}, 0
+    for i in range(size):
+        for j in range(i + 1, size):
+            rows[i, j], rows[j, i] = packed[at : at + 1], -packed[at : at + 1]
+            at += 1
+        rows[i, i] = jnp.zeros_like(packed[:1])
+    return jnp.concatenate([rows[i, j] for i in range(size) for j in range(size)], axis=0)
+
+
+def kernel(n, reps, size, s_ref, v_hbm, out_ref, x, g, dd, v, acc, pb, rrecv, qb, rowrecv, res,
+           lv, a_send, a_recv, l_send, r_send, x_recv, gl_send, gr_send, g_recv, p_send, p_recv, q_send, q_recv,
            o_send, o_recv):
     kb = s_ref.shape[1]
     per_rep = pb.shape[1]
     slots = res.shape[0]
+    off_pairs = n * (n - 1) // 2
+    numbers = off_pairs + -(-n // 2)
+    half = s_ref.shape[2] // 2
+    width = s_ref.shape[3]
+    half_width = min(-(-width // 256) * 128, width)
     r, z, p = lax.axis_index("row"), lax.axis_index("col"), lax.axis_index("rep")
 
     def remote(src, dst, send, recv, **where):
@@ -64,16 +92,47 @@
             shuffle(k, off).start()
         x[k, z, r] = s_ref[r, k]
     acc[...] = jnp.zeros_like(acc)
-    if reps * per_rep != n * (n + 1) // 2:
+    if reps * per_rep != numbers:
         dd[...] = jnp.zeros_like(dd)
 
+    left, right = lax.max(z - 1, 0), lax.min(z + 1, n - 1)
+
     def to_left(k, c):
-        part = x.at[k, c, pl.ds(0, c + 1)]
-        return remote(part, part, l_send.at[k, c], x_recv.at[k, c], col=lax.max(z - 1, 0))
+        part = x.at[k, c, pl.ds(0, c)]
+        return remote(part, part, l_send.at[k, c], x_recv.at[k, c], col=left)
 
     def to_right(k, c):
-        part = x.at[k, c, pl.ds(c, n - c)]
-        return remote(part, part, r_send.at[k, c], x_recv.at[k, c], col=lax.min(z + 1, n - 1))
+        part = x.at[k, c, pl.ds(c + 1, n - 1 - c)]
+        return remote(part, part, r_send.at[k, c], x_recv.at[k, c], col=right)
+
+    def diagonal(m, c):
+        return g.at[c, m] if 2 * m + 1 < kb else g.at[c, m, :, pl.ds(0, half_width)]
+
+    def g_left(m, c):
+        return remote(diagonal(m, c), diagonal(m, c), gl_send.at[m, c], g_recv.at[m, c], col=left)
+
+    def g_right(m, c):
+        return remote(diagonal(m, c), diagonal(m, c), gr_send.at[m, c], g_recv.at[m, c], col=right)
+
+    def pack(m):
+        first = pack_rows(x[2 * m, z, z].astype(jnp.float32), size)
+        if 2 * m + 1 < kb:
+            second = pack_rows(x[2 * m + 1, z, z].astype(jnp.float32), size)
+            g[z, m] = jnp.concatenate([first, second], axis=0).astype(g.dtype)
+        else:
+            tail = first[:, half_width:]
+            fill = jnp.zeros((half, 2 * half_width - width), jnp.float32)
+            tail = jnp.concatenate([tail, fill], axis=1)
+            g[z, m, :, pl.ds(0, half_width)] = jnp.concatenate(
+                [first[:, :half_width], tail], axis=0).astype(g.dtype)
+
+    def unpacked(k, c):
+        m = k // 2
+        if 2 * m + 1 < kb:
+            both = g[c, m].astype(jnp.float32)
+            return both[:half] if k % 2 == 0 else both[half:]
+        both = g[c, m, :, pl.ds(0, half_width)].astype(jnp.float32)
+        return jnp.concatenate([both[:half], both[half:, : width - half_width]], axis=1)
 
     for k in range(kb):
         for off in range(1, n):
@@ -85,23 +144,35 @@
                     to_left(k, c).start()
                 if c < n - 1:
                     to_right(k, c).start()
+        if k % 2 == 1 or k == kb - 1:
+            pack(k // 2)
+            for c in range(n):
+                @pl.when(z == c)
+                def _():
+                    if c > 0:
+                        g_left(k // 2, c).start()
+                    if c < n - 1:
+                        g_right(k // 2, c).start()
+
+    def slot_of(number):
+        return number % reps * per_rep + number // reps
 
     def assemble(k, first, second):
-        number = pair_start(first, n) + second - first
-        slot = lax.rem(number, reps) * per_rep + number // reps
+        slot = slot_of(pair_start(first, n) + second - first - 1)
 
         @pl.when(z <= first)
         def _():
             dd[slot] = x[k, second, first]
 
-        @pl.when((z >= second) & (z > first))
+        @pl.when(z >= second)
         def _():
             dd[slot] = x[k, first, second]
 
-        @pl.when((z > first) & (z < second))
-        def _():
-            dd[slot] = (x[k, second, first].astype(jnp.float32)
-                        - x[k, first, second].astype(jnp.float32)).astype(dd.dtype)
+        if second - first > 1:
+            @pl.when((z > first) & (z < second))
+            def _():
+                dd[slot] = (x[k, second, first].astype(jnp.float32)
+                            - x[k, first, second].astype(jnp.float32)).astype(dd.dtype)
 
     def arrivals(k, d):
         for c in range(n):
@@ -113,6 +184,10 @@
                                       - x[k, c - d, c].astype(jnp.float32)).astype(x.dtype)
                     if c > d:
                         to_left(k, c).start()
+                    if k % 2 == 0:
+                        g_left(k // 2, c).wait_recv()
+                        if c > d:
+                            g_left(k // 2, c).start()
             if c + d < n:
                 @pl.when(z == c + d)
                 def _():
@@ -121,18 +196,23 @@
                                       - x[k, c, c + d].astype(jnp.float32)).astype(x.dtype)
                     if c + d < n - 1:
                         to_right(k, c).start()
+                    if k % 2 == 0:
+                        g_right(k // 2, c).wait_recv()
+                        if c + d < n - 1:
+                            g_right(k // 2, c).start()
 
     for d in range(1, n):
-        @pl.loop(0, kb)
-        def _(k):
+        for k in range(kb):
             arrivals(k, d)
             if d == n - 1:
-                @pl.loop(0, n)
-                def _(first):
-                    @pl.loop(first, n)
-                    def _(second):
+                for first in range(n):
+                    for second in range(first + 1, n):
                         assemble(k, first, second)
-
+                for c in range(0, n, 2):
+                    one = unpacked(k, c)
+                    two = unpacked(k, c + 1) if c + 1 < n else jnp.zeros_like(one)
+                    dd[slot_of(off_pairs + c // 2)] = jnp.concatenate(
+                        [one, two], axis=0).astype(dd.dtype)
                 pltpu.make_async_copy(v_hbm.at[k], v.at[k], lv.at[k]).wait()
                 acc[...] += lax.dot_general(
                     dd[...].reshape(acc.shape[0], dd.shape[2]), v[k],
@@ -171,33 +251,40 @@
 
     mine = r * (1 - 2 * flip) + (n - 1) * flip
 
+    def number_of(s):
+        return (s * n + mine) * reps + p
+
     def deliver(s, do):
-        number = (s * n + mine) * reps + p
+        number = number_of(s)
         first = 0
-        for t in range(1, n):
+        for t in range(1, n - 1):
             first = first + (number >= pair_start(t, n)).astype(jnp.int32)
-        second = number - pair_start(first, n) + first
+        second = number - pair_start(first, n) + first + 1
+        even = 2 * (number - off_pairs)
+        apart = number < off_pairs
+        first, other = jnp.where(apart, first, even), jnp.where(apart, first, even + 1)
+        second, swapped = jnp.where(apart, second, even), jnp.where(apart, second, even + 1)
         for rep in range(reps):
-            for t, (row, col) in enumerate(((first, second), (second, first))):
+            for t, (row, col) in enumerate(((first, second), (swapped, other))):
                 local = (row == r) & (col == z) & (p == rep)
-                wanted = (first != second) if t else (first == first)
+                wanted = (row < n) & (col < n)
 
                 @pl.when(wanted & local)
                 def _():
                     if do == "start":
-                        pltpu.make_async_copy(res.at[s], out_ref.at[z], o_recv.at[z]).start()
+                        pltpu.make_async_copy(res.at[s, t], out_ref.at[z], o_recv.at[z]).start()
 
                 @pl.when(wanted & jnp.logical_not(local))
                 def _():
-                    copy = remote(res.at[s], out_ref.at[z], o_send.at[s, rep, t], o_recv.at[z],
-                                  row=row, col=col, rep=rep)
+                    copy = remote(res.at[s, t], out_ref.at[z], o_send.at[s, rep, t],
+                                  o_recv.at[z], row=row, col=col, rep=rep)
                     if do == "start":
                         copy.start()
                     else:
                         copy.wait_send()
 
     for s in range(slots):
-        @pl.when(s * n + mine < per_rep)
+        @pl.when((s * n + mine < per_rep) & (number_of(s) < numbers))
         def _():
             total = qb[s * n + mine].astype(jnp.float32)
             for off in range(1, n):
@@ -205,7 +292,17 @@
                 remote(rowrecv.at[s, source], rowrecv.at[s, source], q_send.at[0],
                        q_recv.at[s, source], row=source).wait_recv()
                 total += rowrecv[s, source].astype(jnp.float32)
-            res[s] = total.astype(res.dtype)
+
+            @pl.when(number_of(s) < off_pairs)
+            def _():
+                res[s, 0] = total.astype(res.dtype)
+                res[s, 1] = (-swap_rows(total, size)).astype(res.dtype)
+
+            @pl.when(number_of(s) >= off_pairs)
+            def _():
+                res[s, 0] = unpack_rows(total[:half], size).astype(res.dtype)
+                res[s, 1] = unpack_rows(total[half:], size).astype(res.dtype)
+
             deliver(s, "start")
 
     for source in range(n):
@@ -213,7 +310,7 @@
                col=source).wait_recv()
 
     for s in range(slots):
-        @pl.when(s * n + mine < per_rep)
+        @pl.when((s * n + mine < per_rep) & (number_of(s) < numbers))
         def _():
             deliver(s, "wait")
     for q in range(per_rep):
@@ -237,20 +334,34 @@
                 def _():
                     to_right(k, c).wait_send()
 
-
-def ladder_blocks(staged, integrals, n, reps):
+    for m in range(-(-kb // 2)):
+        for c in range(n):
+            if c > 0:
+                @pl.when((z <= c) & (z > 0))
+                def _():
+                    g_left(m, c).wait_send()
+            if c < n - 1:
+                @pl.when((z >= c) & (z < n - 1))
+                def _():
+                    g_right(m, c).wait_send()
+
+
+def ladder_blocks(staged, integrals, n, reps, size):
     kb, rows, width = staged.shape[1:]
     slab_rows = integrals.shape[1]
-    per_rep = -(-(n * (n + 1) // 2) // reps)
+    numbers = n * (n - 1) // 2 + -(-n // 2)
+    chunks = -(-kb // 2)
+    per_rep = -(-numbers // reps)
     slots = -(-per_rep // n)
     bf16, dma = jnp.bfloat16, pltpu.SemaphoreType.DMA
     return pl.pallas_call(
-        functools.partial(kernel, n, reps),
+        functools.partial(kernel, n, reps, size),
         out_shape=jax.ShapeDtypeStruct((n, rows, slab_rows), bf16),
         in_specs=[pl.BlockSpec(memory_space=pltpu.VMEM), pl.BlockSpec(memory_space=pl.ANY)],
         out_specs=pl.BlockSpec(memory_space=pl.ANY),
         scratch_shapes=[
             pltpu.VMEM((kb, n, n, rows, width), bf16),
+            pltpu.VMEM((n, chunks, rows, width), bf16),
             pltpu.VMEM((reps * per_rep, rows, width), bf16),
             pltpu.VMEM((kb, slab_rows, width), bf16),
             pltpu.VMEM((reps * per_rep * rows, slab_rows), jnp.float32),
@@ -258,13 +369,16 @@
             pltpu.VMEM((max(reps - 1, 1), per_rep, rows, slab_rows), bf16),
             pltpu.VMEM((per_rep, rows, slab_rows), bf16),
             pltpu.VMEM((slots, n, rows, slab_rows), bf16),
-            pltpu.VMEM((slots, rows, slab_rows), bf16),
+            pltpu.VMEM((slots, 2, rows, slab_rows), bf16),
             dma((kb,)),
             dma((kb, n - 1)),
             dma((kb, n - 1)),
             dma((kb, n)),
             dma((kb, n)),
             dma((kb, n)),
+            dma((chunks, n)),
+            dma((chunks, n)),
+            dma((chunks, n)),
             dma((max(reps - 1, 1),)),
             dma((max(reps - 1, 1),)),
             dma((per_rep,)),
@@ -286,11 +400,10 @@
     mixed = (natural.astype(jnp.float32) - swapped.astype(jnp.float32)).astype(natural.dtype)
     staged = jnp.where(r < z, natural, jnp.where(r > z, swapped, mixed))
     staged = staged.reshape(n, kb, block * block, pairs // n)
-    blocks = ladder_blocks(staged, jnp.transpose(integrals, (1, 0, 2)), n, reps)
+    blocks = ladder_blocks(staged, jnp.transpose(integrals, (1, 0, 2)), n, reps, block)
     slab_rows = integrals.shape[0]
     found = jnp.transpose(blocks.reshape(n, block, block, slab_rows), (1, 2, 0, 3))
     found = found.reshape(block, block, n * slab_rows)
-    found = jnp.where(r <= z, found, -jnp.swapaxes(found, 0, 1))
     row_orbitals = r * block + jnp.arange(block, dtype=jnp.int32)
     col_orbitals = z * block + jnp.arange(block, dtype=jnp.int32)
     target = jnp.bitwise_xor(slab[0], slab[1])

time: 63.3 us -> 62.7 us (level)
  the two profiles are of different devices: /device:TPU:0 before, /device:TPU:1 now
where the time goes in v3:
time: 62.7 us; the launch traced here: 62.5 us
  Pallas kernels  53.6 us (85%)
  local copies, waits for them, and re-layouts  5.32 us (8%)
  other arithmetic  2.19 us (3%)
  between operations  1.39 us (2%)
    pallas_call x1, Pallas kernels, ladder_blocks(): pl.pallas_call(functools.partial(kernel, n, reps, size), out_shape=jax.Sh...  53.6 us
    reshape x1, local copies, waits for them, and re-layouts, shards(): amplitudes.reshape(block, block, kb, n, pairs // n)  1.7 us
    slice x1, local copies, waits for them, and re-layouts, shards(): target = jnp.bitwise_xor(slab[0], slab[1])  1.33 us

profile of v3, /device:TPU:1, one launch (start us, length us, event | category | flops | bytes accessed | tf_op | source)
XLA Modules:
  0.0 62.5 jit_solution(11088034069130016797)
XLA Ops:
  0.0 0.9 %convert_reduce_fusion.1 = (s32[4]{0:T(128)S(1)}, s32[4]{0:T(128)S(1)}) fusion(s32[9]{0:T(128)} %param.6, pred[9]{0:T(512)(128)(4,1)S(1)} %compare_and_fusion, s32[4]{0:T(128)S(1)} %get-tuple-element.10, s32[4]{0:T(128)S(1)} %get-tuple-element.9), kind=kLoop, calls=%fused_computation.6 | loop fusion | flops 280 | bytes 109 | tf_op jit(solution)/shard_map/reduce_sum | solution.py:16
  0.9 1.3 %fusion.2 = (s32[1]{0:T(128)}, s32[1]{0:T(128)}) fusion(s32[2]{0:T(128)} %param.7), kind=kLoop, calls=%fused_computation.10 | loop fusion | bytes 16 | tf_op jit(solution)/shard_map/slice | solution.py:409
  3.6 0.1 xor_compare_fusion
  3.6 1.7 %reshape.57 = bf16[4,4,3,4,1296]{4,3,1,2,0:T(4,128)(2,1)S(1)} reshape(bf16[4,4,3,5184]{3,1,2,0:T(4,128)(2,1)} %param.4) | data formatting | bytes 995328 | tf_op jit(solution)/shard_map/reshape | solution.py:398
  5.3 0.4 fusion.1
  5.8 1.0 %reshape.58.s_ref = bf16[4,3,16,1296]{3,2,1,0:T(8,128)(2,1)} reshape(bf16[4,3,4,4,1296]{4,3,2,1,0:T(4,128)(2,1)S(1)} %fusion.1) | data formatting | bytes 995328 | tf_op jit(solution)/shard_map/reshape | solution.py:402
  6.8 53.6 %ladder_blocks.1 = bf16[4,16,1296]{2,1,0:T(8,128)(2,1)} custom-call(bf16[4,3,16,1296]{3,2,1,0:T(8,128)(2,1)} %reshape.58.s_ref, bf16[3,1296,1296]{2,1,0:T(8,128)(2,1)} %bitcast.9), custom_call_target="tpu_custom_call" | custom-call | tf_op jit(solution)/shard_map/ladder_blocks/pallas_call | solution.py:357
  60.4 1.0 %reshape.59 = bf16[4,4,4,1296]{3,2,1,0:T(4,128)(2,1)S(1)} reshape(bf16[4,16,1296]{2,1,0:T(8,128)(2,1)} %ladder_blocks.1) | data formatting | bytes 331776 | tf_op jit(solution)/shard_map/reshape | solution.py:405
  61.4 0.1 copy.10
  61.5 0.2 reshape.60
  61.7 0.8 %broadcast_select_fusion = bf16[4,4,5184]{2,1,0:T(4,128)(2,1)} fusion(bf16[4,4,5184]{2,1,0:T(4,128)(2,1)S(1)} %reshape.60, pred[4,4]{1,0:T(4,128)(4,1)S(1)} %xor_compare_fusion), kind=kLoop, calls=%fused_computation.3 | loop fusion | flops 82944 | bytes 331792 | tf_op jit(solution)/shard_map/jit(_where)/select_n | solution.py:413
  (2 shorter events, 0.0 us)

commit v4 on v3

--- a/solution.py
+++ b/solution.py
@@ -8,12 +8,6 @@
 from jax.sharding import PartitionSpec as P
 
 MESH = pl.DeviceIdType.MESH
-
-
-def irrep_labels(orbitals, occ_offsets):
-    bound = jnp.arange(occ_offsets.shape[0], dtype=jnp.int32)
-    inner = (bound >= 1) & (bound < occ_offsets.shape[0] - 1)
-    return jnp.sum(((orbitals[:, None] >= occ_offsets[None, :]) & inner[None, :]).astype(jnp.int32), axis=1)
 
 
 def pair_start(first, n):
@@ -41,10 +35,11 @@
     return jnp.concatenate([rows[i, j] for i in range(size) for j in range(size)], axis=0)
 
 
-def kernel(n, reps, size, s_ref, v_hbm, out_ref, x, g, dd, v, acc, pb, rrecv, qb, rowrecv, res,
+def kernel(n, reps, size, a_ref, v_hbm, occ_ref, slab_ref, out_ref, s_ref, found, x, g, dd, v, acc, pb, rrecv, qb, rowrecv, res,
            lv, a_send, a_recv, l_send, r_send, x_recv, gl_send, gr_send, g_recv, p_send, p_recv, q_send, q_recv,
            o_send, o_recv):
     kb = s_ref.shape[1]
+    f32 = jnp.float32
     per_rep = pb.shape[1]
     slots = res.shape[0]
     off_pairs = n * (n - 1) // 2
@@ -75,8 +70,6 @@
             device_id=(other // (n * reps), lax.rem(other // reps, n), lax.rem(other, reps)),
             device_id_type=MESH)
 
-    pl.semaphore_wait(barrier, devices - 1)
-
     def shuffle(k, off):
         dest = lax.rem(r + off, n)
         return remote(s_ref.at[dest, k], x.at[k, z, r], a_send.at[k, off - 1],
@@ -87,13 +80,35 @@
         return remote(s_ref.at[source, k], x.at[k, z, source], a_send.at[k, off - 1],
                       a_recv.at[k, off - 1], row=source)
 
+    def stage(k):
+        for dest in range(n):
+            natural = jnp.concatenate(
+                [a_ref[i, k, :, dest * width : (dest + 1) * width].astype(f32) for i in range(size)],
+                axis=0)
+
+            @pl.when(r < z)
+            def _():
+                s_ref[dest, k] = natural.astype(s_ref.dtype)
+
+            @pl.when(r > z)
+            def _():
+                s_ref[dest, k] = swap_rows(natural, size).astype(s_ref.dtype)
+
+            @pl.when(r == z)
+            def _():
+                s_ref[dest, k] = (natural - swap_rows(natural, size)).astype(s_ref.dtype)
+
+    stage(0)
+    acc[...] = jnp.zeros_like(acc)
+    if reps * per_rep != numbers:
+        dd[...] = jnp.zeros_like(dd)
+    pl.semaphore_wait(barrier, devices - 1)
     for k in range(kb):
         for off in range(1, n):
             shuffle(k, off).start()
         x[k, z, r] = s_ref[r, k]
-    acc[...] = jnp.zeros_like(acc)
-    if reps * per_rep != numbers:
-        dd[...] = jnp.zeros_like(dd)
+        if k + 1 < kb:
+            stage(k + 1)
 
     left, right = lax.max(z - 1, 0), lax.min(z + 1, n - 1)
 
@@ -215,10 +230,10 @@
                         [one, two], axis=0).astype(dd.dtype)
                 pltpu.make_async_copy(v_hbm.at[k], v.at[k], lv.at[k]).wait()
                 acc[...] += lax.dot_general(
-                    dd[...].reshape(acc.shape[0], dd.shape[2]), v[k],
+                    v[k], dd[...].reshape(acc.shape[1], dd.shape[2]),
                     (((1,), (1,)), ((), ())), preferred_element_type=jnp.float32)
 
-    pb[...] = acc[...].reshape(pb.shape).astype(pb.dtype)
+    pb[...] = acc[...].T.reshape(pb.shape).astype(pb.dtype)
 
     def swap_reps(off):
         other = lax.rem(p + off, reps)
@@ -251,10 +266,24 @@
 
     mine = r * (1 - 2 * flip) + (n - 1) * flip
 
+    place = lax.broadcasted_iota(jnp.int32, (size * size, 128), 0)
+    place_i = sum((place >= t * size).astype(jnp.int32) for t in range(1, size))
+    place_j = place - size * place_i
+    target = jnp.bitwise_xor(slab_ref[0], slab_ref[1])
+
+    def labels(orbitals):
+        return sum((orbitals >= occ_ref[t]).astype(jnp.int32)
+                   for t in range(1, occ_ref.shape[0] - 1))
+
+    def masked(block, first, second):
+        mixed = jnp.bitwise_xor(labels(first * size + place_i), labels(second * size + place_j))
+        allowed = (mixed == target).astype(f32)[:, :1]
+        return jnp.where(jnp.broadcast_to(allowed, block.shape) > 0, block, jnp.zeros_like(block))
+
     def number_of(s):
         return (s * n + mine) * reps + p
 
-    def deliver(s, do):
+    def blocks_of(s):
         number = number_of(s)
         first = 0
         for t in range(1, n - 1):
@@ -264,6 +293,10 @@
         apart = number < off_pairs
         first, other = jnp.where(apart, first, even), jnp.where(apart, first, even + 1)
         second, swapped = jnp.where(apart, second, even), jnp.where(apart, second, even + 1)
+        return first, second, other, swapped
+
+    def deliver(s, do):
+        first, second, other, swapped = blocks_of(s)
         for rep in range(reps):
             for t, (row, col) in enumerate(((first, second), (swapped, other))):
                 local = (row == r) & (col == z) & (p == rep)
@@ -272,11 +305,11 @@
                 @pl.when(wanted & local)
                 def _():
                     if do == "start":
-                        pltpu.make_async_copy(res.at[s, t], out_ref.at[z], o_recv.at[z]).start()
+                        pltpu.make_async_copy(res.at[s, t], found.at[z], o_recv.at[z]).start()
 
                 @pl.when(wanted & jnp.logical_not(local))
                 def _():
-                    copy = remote(res.at[s, t], out_ref.at[z], o_send.at[s, rep, t],
+                    copy = remote(res.at[s, t], found.at[z], o_send.at[s, rep, t],
                                   o_recv.at[z], row=row, col=col, rep=rep)
                     if do == "start":
                         copy.start()
@@ -293,21 +326,28 @@
                        q_recv.at[s, source], row=source).wait_recv()
                 total += rowrecv[s, source].astype(jnp.float32)
 
+            first, second, other, _swapped = blocks_of(s)
+
             @pl.when(number_of(s) < off_pairs)
             def _():
-                res[s, 0] = total.astype(res.dtype)
-                res[s, 1] = (-swap_rows(total, size)).astype(res.dtype)
+                kept = masked(total, first, second)
+                res[s, 0] = kept.astype(res.dtype)
+                res[s, 1] = (-swap_rows(kept, size)).astype(res.dtype)
 
             @pl.when(number_of(s) >= off_pairs)
             def _():
-                res[s, 0] = unpack_rows(total[:half], size).astype(res.dtype)
-                res[s, 1] = unpack_rows(total[half:], size).astype(res.dtype)
+                res[s, 0] = masked(unpack_rows(total[:half], size), first, first).astype(res.dtype)
+                res[s, 1] = masked(unpack_rows(total[half:], size), other, other).astype(res.dtype)
 
             deliver(s, "start")
 
     for source in range(n):
-        remote(out_ref.at[source], out_ref.at[source], o_send.at[0, 0, 0], o_recv.at[source],
+        remote(found.at[source], found.at[source], o_send.at[0, 0, 0], o_recv.at[source],
                col=source).wait_recv()
+
+    whole = jnp.concatenate([found[source].astype(f32) for source in range(n)], axis=1)
+    for i in range(size):
+        out_ref[i] = whole[i * size : (i + 1) * size].astype(out_ref.dtype)
 
     for s in range(slots):
         @pl.when((s * n + mine < per_rep) & (number_of(s) < numbers))
@@ -346,8 +386,9 @@
                     g_right(m, c).wait_send()
 
 
-def ladder_blocks(staged, integrals, n, reps, size):
-    kb, rows, width = staged.shape[1:]
+def ladder_blocks(amplitudes, integrals, occ_offsets, slab, n, reps):
+    size, kb, _, pairs = amplitudes.shape
+    rows, width = size * size, pairs // n
     slab_rows = integrals.shape[1]
     numbers = n * (n - 1) // 2 + -(-n // 2)
     chunks = -(-kb // 2)
@@ -356,15 +397,22 @@
     bf16, dma = jnp.bfloat16, pltpu.SemaphoreType.DMA
     return pl.pallas_call(
         functools.partial(kernel, n, reps, size),
-        out_shape=jax.ShapeDtypeStruct((n, rows, slab_rows), bf16),
-        in_specs=[pl.BlockSpec(memory_space=pltpu.VMEM), pl.BlockSpec(memory_space=pl.ANY)],
-        out_specs=pl.BlockSpec(memory_space=pl.ANY),
+        out_shape=jax.ShapeDtypeStruct((size, size, n * slab_rows), bf16),
+        in_specs=[
+            pl.BlockSpec(memory_space=pltpu.VMEM),
+            pl.BlockSpec(memory_space=pl.ANY),
+            pl.BlockSpec(memory_space=pltpu.SMEM),
+            pl.BlockSpec(memory_space=pltpu.SMEM),
+        ],
+        out_specs=pl.BlockSpec(memory_space=pltpu.VMEM),
         scratch_shapes=[
+            pltpu.VMEM((n, kb, rows, width), bf16),
+            pltpu.VMEM((n, rows, slab_rows), bf16),
             pltpu.VMEM((kb, n, n, rows, width), bf16),
             pltpu.VMEM((n, chunks, rows, width), bf16),
             pltpu.VMEM((reps * per_rep, rows, width), bf16),
             pltpu.VMEM((kb, slab_rows, width), bf16),
-            pltpu.VMEM((reps * per_rep * rows, slab_rows), jnp.float32),
+            pltpu.VMEM((slab_rows, reps * per_rep * rows), jnp.float32),
             pltpu.VMEM((reps, per_rep, rows, slab_rows), bf16),
             pltpu.VMEM((max(reps - 1, 1), per_rep, rows, slab_rows), bf16),
             pltpu.VMEM((per_rep, rows, slab_rows), bf16),
@@ -389,28 +437,13 @@
         compiler_params=pltpu.CompilerParams(
             collective_id=0, has_side_effects=True, vmem_limit_bytes=56 * 1024 * 1024),
         name="ladder_blocks",
-    )(staged, integrals)
+    )(amplitudes, integrals, occ_offsets, slab)
 
 
 def shards(n, reps, amplitudes, integrals, occ_offsets, slab):
-    block, _, kb, pairs = amplitudes.shape
-    r, z = lax.axis_index("row"), lax.axis_index("col")
-    natural = jnp.transpose(amplitudes.reshape(block, block, kb, n, pairs // n), (3, 2, 0, 1, 4))
-    swapped = jnp.swapaxes(natural, 2, 3)
-    mixed = (natural.astype(jnp.float32) - swapped.astype(jnp.float32)).astype(natural.dtype)
-    staged = jnp.where(r < z, natural, jnp.where(r > z, swapped, mixed))
-    staged = staged.reshape(n, kb, block * block, pairs // n)
-    blocks = ladder_blocks(staged, jnp.transpose(integrals, (1, 0, 2)), n, reps, block)
-    slab_rows = integrals.shape[0]
-    found = jnp.transpose(blocks.reshape(n, block, block, slab_rows), (1, 2, 0, 3))
-    found = found.reshape(block, block, n * slab_rows)
-    row_orbitals = r * block + jnp.arange(block, dtype=jnp.int32)
-    col_orbitals = z * block + jnp.arange(block, dtype=jnp.int32)
-    target = jnp.bitwise_xor(slab[0], slab[1])
-    row_labels = irrep_labels(row_orbitals, occ_offsets)
-    col_labels = irrep_labels(col_orbitals, occ_offsets)
-    allowed = jnp.bitwise_xor(row_labels[:, None], col_labels[None, :]) == target
-    return jnp.where(allowed[:, :, None], found, jnp.bfloat16(0.0))
+    return ladder_blocks(
+        jnp.transpose(amplitudes, (0, 2, 1, 3)), jnp.transpose(integrals, (1, 0, 2)),
+        occ_offsets, slab, n, reps)
 
 
 def solution(mesh):

time: 62.7 us -> 58.4 us (0.931)
  local copies, waits for them, and re-layouts: 5.32 us -> 1.64 us
  Pallas kernels: 53.6 us -> 56.6 us
  other arithmetic: 2.19 us -> 0 us
  between operations: 1.39 us -> 0.01 us
    reshape x4 -> x0, local copies, waits for them, and re-layouts: 3.92 us -> none  [the longest x1 1.7 us: shards(): amplitudes.reshape(block, block, kb, n, pairs // n)]
    pallas_call x1, Pallas kernels: 53.6 us -> 56.6 us  [ladder_blocks(): pl.pallas_call(functools.partial(kernel, n, reps, size), out_shape=jax.Sh...]
    unnamed x0 -> x1, local copies, waits for them, and re-layouts: none -> 1.64 us
    slice x1 -> x0, local copies, waits for them, and re-layouts: 1.33 us -> none  [shards(): target = jnp.bitwise_xor(slab[0], slab[1])]
    select_n x2 -> x0, other arithmetic: 1.23 us -> none  [the longest x1 0.81 us: shards(): return jnp.where(allowed[:, :, None], found, jnp.bfloat16(0.0))]
    reduce_sum x1 -> x0, other arithmetic: 0.87 us -> none  [irrep_labels(): jnp.sum(((orbitals[:, None] >= occ_offsets[None, :]) & inner[None, :]).as...]
where the time goes in v4:
time: 58.4 us; the launch traced here: 58.2 us
  Pallas kernels  56.6 us (97%)
  local copies, waits for them, and re-layouts  1.64 us (3%)
    pallas_call x1, Pallas kernels, ladder_blocks(): pl.pallas_call(functools.partial(kernel, n, reps, size), out_shape=jax.Sh...  56.6 us
    unnamed x1, local copies, waits for them, and re-layouts  1.64 us

profile of v4, /device:TPU:1, one launch (start us, length us, event | category | flops | bytes accessed | tf_op | source)
XLA Modules:
  0.0 58.2 jit_solution(6981614314441920696)
XLA Ops:
  0.0 56.6 %ladder_blocks.1 = bf16[4,4,5184]{2,1,0:T(4,128)(2,1)} custom-call(bf16[4,3,4,5184]{3,2,1,0:T(4,128)(2,1)} %bitcast.3, bf16[3,1296,1296]{2,1,0:T(8,128)(2,1)} %bitcast.2, s32[9]{0:T(128)} %occ_ref.1, s32[2]{0:T(128)} %slab_ref.1), custom_call_target="tpu_custom_call" | custom-call | tf_op jit(solution)/shard_map/ladder_blocks/pallas_call | solution.py:398
  56.6 1.6 %copy.6 = bf16[4,4,5184]{2,1,0:T(4,128)(2,1)} copy(bf16[4,4,5184]{2,1,0:T(4,128)(2,1)} %ladder_blocks.1) | data formatting | bytes 331776

commit v5 on v4

--- a/solution.py
+++ b/solution.py
@@ -35,8 +35,8 @@
     return jnp.concatenate([rows[i, j] for i in range(size) for j in range(size)], axis=0)
 
 
-def kernel(n, reps, size, a_ref, v_hbm, occ_ref, slab_ref, out_ref, s_ref, found, x, g, dd, v, acc, pb, rrecv, qb, rowrecv, res,
-           lv, a_send, a_recv, l_send, r_send, x_recv, gl_send, gr_send, g_recv, p_send, p_recv, q_send, q_recv,
+def kernel(n, reps, size, a_hbm, v_hbm, occ_ref, slab_ref, out_ref, a_ref, s_ref, found, x, g, dd, v, acc, pb, rrecv, qb, rowrecv, res,
+           la, lv, a_send, a_recv, l_send, r_send, x_recv, gl_send, gr_send, g_recv, p_send, p_recv, q_send, q_recv,
            o_send, o_recv):
     kb = s_ref.shape[1]
     f32 = jnp.float32
@@ -55,6 +55,8 @@
             src_ref=src, dst_ref=dst, send_sem=send, recv_sem=recv,
             device_id=(target["row"], target["col"], target["rep"]), device_id_type=MESH)
 
+    fetch = pltpu.make_async_copy(a_hbm, a_ref, la)
+    fetch.start()
     for k in range(kb):
         pltpu.make_async_copy(v_hbm.at[k], v.at[k], lv.at[k]).start()
 
@@ -98,17 +100,21 @@
             def _():
                 s_ref[dest, k] = (natural - swap_rows(natural, size)).astype(s_ref.dtype)
 
+    acc[...] = jnp.zeros_like(acc)
+    fetch.wait()
     stage(0)
-    acc[...] = jnp.zeros_like(acc)
     if reps * per_rep != numbers:
         dd[...] = jnp.zeros_like(dd)
     pl.semaphore_wait(barrier, devices - 1)
-    for k in range(kb):
+    def send_shuffle(k):
         for off in range(1, n):
             shuffle(k, off).start()
         x[k, z, r] = s_ref[r, k]
-        if k + 1 < kb:
-            stage(k + 1)
+
+    send_shuffle(0)
+    if kb > 1:
+        stage(1)
+        send_shuffle(1)
 
     left, right = lax.max(z - 1, 0), lax.min(z + 1, n - 1)
 
@@ -159,6 +165,9 @@
                     to_left(k, c).start()
                 if c < n - 1:
                     to_right(k, c).start()
+        if k + 2 < kb:
+            stage(k + 2)
+            send_shuffle(k + 2)
         if k % 2 == 1 or k == kb - 1:
             pack(k // 2)
             for c in range(n):
@@ -183,11 +192,10 @@
         def _():
             dd[slot] = x[k, first, second]
 
-        if second - first > 1:
-            @pl.when((z > first) & (z < second))
-            def _():
-                dd[slot] = (x[k, second, first].astype(jnp.float32)
-                            - x[k, first, second].astype(jnp.float32)).astype(dd.dtype)
+        @pl.when((z > first) & (z < second))
+        def _():
+            dd[slot] = (x[k, second, first].astype(f32)
+                        - x[k, first, second].astype(f32)).astype(dd.dtype)
 
     def arrivals(k, d):
         for c in range(n):
@@ -195,43 +203,61 @@
                 @pl.when(z == c - d)
                 def _():
                     to_left(k, c).wait_recv()
-                    x[k, c, c - d] = (x[k, c, c - d].astype(jnp.float32)
-                                      - x[k, c - d, c].astype(jnp.float32)).astype(x.dtype)
+                    x[k, c, c - d] = (x[k, c, c - d].astype(f32)
+                                      - x[k, c - d, c].astype(f32)).astype(x.dtype)
                     if c > d:
                         to_left(k, c).start()
-                    if k % 2 == 0:
-                        g_left(k // 2, c).wait_recv()
-                        if c > d:
-                            g_left(k // 2, c).start()
+                    for m in range(-(-kb // 2)):
+                        @pl.when(k == 2 * m)
+                        def _():
+                            g_left(m, c).wait_recv()
+                            if c > d:
+                                g_left(m, c).start()
             if c + d < n:
                 @pl.when(z == c + d)
                 def _():
                     to_right(k, c).wait_recv()
-                    x[k, c, c + d] = (x[k, c + d, c].astype(jnp.float32)
-                                      - x[k, c, c + d].astype(jnp.float32)).astype(x.dtype)
+                    x[k, c, c + d] = (x[k, c + d, c].astype(f32)
+                                      - x[k, c, c + d].astype(f32)).astype(x.dtype)
                     if c + d < n - 1:
                         to_right(k, c).start()
-                    if k % 2 == 0:
-                        g_right(k // 2, c).wait_recv()
-                        if c + d < n - 1:
-                            g_right(k // 2, c).start()
-
-    for d in range(1, n):
-        for k in range(kb):
-            arrivals(k, d)
-            if d == n - 1:
-                for first in range(n):
-                    for second in range(first + 1, n):
-                        assemble(k, first, second)
+                    for m in range(-(-kb // 2)):
+                        @pl.when(k == 2 * m)
+                        def _():
+                            g_right(m, c).wait_recv()
+                            if c + d < n - 1:
+                                g_right(m, c).start()
+
+    def multiply(k):
+        @pl.loop(0, n - 1)
+        def _(first):
+            @pl.loop(first + 1, n)
+            def _(second):
+                assemble(k, first, second)
+
+        for now in range(kb):
+            @pl.when(k == now)
+            def _():
                 for c in range(0, n, 2):
-                    one = unpacked(k, c)
-                    two = unpacked(k, c + 1) if c + 1 < n else jnp.zeros_like(one)
+                    one = unpacked(now, c)
+                    two = unpacked(now, c + 1) if c + 1 < n else jnp.zeros_like(one)
                     dd[slot_of(off_pairs + c // 2)] = jnp.concatenate(
                         [one, two], axis=0).astype(dd.dtype)
-                pltpu.make_async_copy(v_hbm.at[k], v.at[k], lv.at[k]).wait()
-                acc[...] += lax.dot_general(
-                    v[k], dd[...].reshape(acc.shape[1], dd.shape[2]),
-                    (((1,), (1,)), ((), ())), preferred_element_type=jnp.float32)
+
+        pltpu.make_async_copy(v_hbm.at[k], v.at[k], lv.at[k]).wait()
+        acc[...] += lax.dot_general(
+            v[k], dd[...].reshape(acc.shape[1], dd.shape[2]),
+            (((1,), (1,)), ((), ())), preferred_element_type=f32)
+
+    last = lax.max(z, n - 1 - z)
+    for d in range(1, n):
+        @pl.loop(0, kb)
+        def _(k):
+            arrivals(k, d)
+            if 2 * d >= n - 1:
+                @pl.when(d == last)
+                def _():
+                    multiply(k)
 
     pb[...] = acc[...].T.reshape(pb.shape).astype(pb.dtype)
 
@@ -347,7 +373,7 @@
 
     whole = jnp.concatenate([found[source].astype(f32) for source in range(n)], axis=1)
     for i in range(size):
-        out_ref[i] = whole[i * size : (i + 1) * size].astype(out_ref.dtype)
+        out_ref[i] = -whole[i * size : (i + 1) * size].astype(out_ref.dtype)
 
     for s in range(slots):
         @pl.when((s * n + mine < per_rep) & (number_of(s) < numbers))
@@ -399,13 +425,14 @@
         functools.partial(kernel, n, reps, size),
         out_shape=jax.ShapeDtypeStruct((size, size, n * slab_rows), bf16),
         in_specs=[
-            pl.BlockSpec(memory_space=pltpu.VMEM),
+            pl.BlockSpec(memory_space=pl.ANY),
             pl.BlockSpec(memory_space=pl.ANY),
             pl.BlockSpec(memory_space=pltpu.SMEM),
             pl.BlockSpec(memory_space=pltpu.SMEM),
         ],
         out_specs=pl.BlockSpec(memory_space=pltpu.VMEM),
         scratch_shapes=[
+            pltpu.VMEM(amplitudes.shape[:1] + (kb, size, pairs), bf16),
             pltpu.VMEM((n, kb, rows, width), bf16),
             pltpu.VMEM((n, rows, slab_rows), bf16),
             pltpu.VMEM((kb, n, n, rows, width), bf16),
@@ -418,6 +445,7 @@
             pltpu.VMEM((per_rep, rows, slab_rows), bf16),
             pltpu.VMEM((slots, n, rows, slab_rows), bf16),
             pltpu.VMEM((slots, 2, rows, slab_rows), bf16),
+            dma,
             dma((kb,)),
             dma((kb, n - 1)),
             dma((kb, n - 1)),
@@ -441,7 +469,7 @@
 
 
 def shards(n, reps, amplitudes, integrals, occ_offsets, slab):
-    return ladder_blocks(
+    return -ladder_blocks(
         jnp.transpose(amplitudes, (0, 2, 1, 3)), jnp.transpose(integrals, (1, 0, 2)),
         occ_offsets, slab, n, reps)
 

time: 58.4 us -> 54.9 us (0.940)
  Pallas kernels: 56.6 us -> 53.1 us
  other arithmetic: 0 us -> 1.66 us
  local copies, waits for them, and re-layouts: 1.64 us -> 0 us
    pallas_call x1, Pallas kernels: 56.6 us -> 53.1 us  [ladder_blocks(): pl.pallas_call(functools.partial(kernel, n, reps, size), out_shape=jax.Sh...]
    neg x0 -> x1, other arithmetic: none -> 1.66 us  [shards(): -ladder_blocks(jnp.transpose(amplitudes, (0, 2, 1, 3)), jnp.transpose(int...]
    unnamed x1 -> x0, local copies, waits for them, and re-layouts: 1.64 us -> none
where the time goes in v5:
time: 54.9 us; the launch traced here: 54.7 us
  Pallas kernels  53.1 us (97%)
  other arithmetic  1.66 us (3%)
    pallas_call x1, Pallas kernels, ladder_blocks(): pl.pallas_call(functools.partial(kernel, n, reps, size), out_shape=jax.Sh...  53.1 us
    neg x1, other arithmetic, shards(): -ladder_blocks(jnp.transpose(amplitudes, (0, 2, 1, 3)), jnp.transpose(int...  1.66 us

profile of v5, /device:TPU:1, one launch (start us, length us, event | category | flops | bytes accessed | tf_op | source)
XLA Modules:
  0.0 54.7 jit_solution(1682866016118668340)
XLA Ops:
  0.0 53.1 %ladder_blocks.1 = bf16[4,4,5184]{2,1,0:T(4,128)(2,1)} custom-call(bf16[4,3,4,5184]{3,2,1,0:T(4,128)(2,1)} %bitcast.3, bf16[3,1296,1296]{2,1,0:T(8,128)(2,1)} %bitcast.2, s32[9]{0:T(128)} %occ_ref.1, s32[2]{0:T(128)} %slab_ref.1), custom_call_target="tpu_custom_call" | custom-call | tf_op jit(solution)/shard_map/ladder_blocks/pallas_call | solution.py:424
  53.1 1.7 %neg.3 = bf16[4,4,5184]{2,1,0:T(4,128)(2,1)} negate(bf16[4,4,5184]{2,1,0:T(4,128)(2,1)} %ladder_blocks.1) | non-fusion elementwise | flops 82944 | bytes 331776 | tf_op jit(solution)/shard_map/neg | solution.py:472

commit v6 on v5

--- a/solution.py
+++ b/solution.py
@@ -14,25 +14,28 @@
     return first * (n - 1) - first * (first - 1) // 2
 
 
-def swap_rows(block, size):
-    return jnp.concatenate(
-        [block[i * size + j : i * size + j + 1] for j in range(size) for i in range(size)], axis=0)
-
-
 def pack_rows(block, size):
     above = [block[i * size + i + 1 : (i + 1) * size] for i in range(size - 1)]
     rest = size * size // 2 - size * (size - 1) // 2
     return jnp.concatenate(above + [jnp.zeros_like(block[:rest])], axis=0)
 
 
-def unpack_rows(packed, size):
-    rows, at = {}, 0
-    for i in range(size):
-        for j in range(i + 1, size):
-            rows[i, j], rows[j, i] = packed[at : at + 1], -packed[at : at + 1]
-            at += 1
-        rows[i, i] = jnp.zeros_like(packed[:1])
-    return jnp.concatenate([rows[i, j] for i in range(size) for j in range(size)], axis=0)
+def row_orders(size):
+    rows = size * size
+    row = lax.broadcasted_iota(jnp.int32, (rows, rows), 0)
+    column = lax.broadcasted_iota(jnp.int32, (rows, rows), 1)
+    i = sum((row >= t * size).astype(jnp.int32) for t in range(1, size))
+    j = row - size * i
+    low, high = jnp.minimum(i, j), jnp.maximum(i, j)
+    at = low * size + high - low - 1 - sum(jnp.where(low >= t, t, 0) for t in range(1, size))
+    sign = jnp.where(i < j, 1.0, -1.0)
+
+    def packed(start):
+        return jnp.where((i != j) & (column == at + start), sign, 0.0)
+
+    same = jnp.where(row == column, 1.0, 0.0)
+    swapped = jnp.where(column == j * size + i, 1.0, 0.0)
+    return same, swapped, packed(0), packed(rows // 2)
 
 
 def kernel(n, reps, size, a_hbm, v_hbm, occ_ref, slab_ref, out_ref, a_ref, s_ref, found, x, g, dd, v, acc, pb, rrecv, qb, rowrecv, res,
@@ -46,6 +49,11 @@
     numbers = off_pairs + -(-n // 2)
     half = s_ref.shape[2] // 2
     width = s_ref.shape[3]
+    piece = v.shape[2]
+    same, swapped_rows, packed_first, packed_second = row_orders(size)
+
+    def reorder(matrix, block):
+        return jnp.dot(matrix.astype(jnp.bfloat16), block, preferred_element_type=f32)
     half_width = min(-(-width // 256) * 128, width)
     r, z, p = lax.axis_index("row"), lax.axis_index("col"), lax.axis_index("rep")
 
@@ -83,22 +91,16 @@
                       a_recv.at[k, off - 1], row=source)
 
     def stage(k):
+        natural = jnp.concatenate([a_ref[i, k].astype(f32) for i in range(size)], axis=0)
+        order = jnp.where(r < z, same, jnp.where(r > z, swapped_rows, same - swapped_rows))
+        staged = reorder(order, natural.astype(s_ref.dtype)).astype(s_ref.dtype)
         for dest in range(n):
-            natural = jnp.concatenate(
-                [a_ref[i, k, :, dest * width : (dest + 1) * width].astype(f32) for i in range(size)],
-                axis=0)
-
-            @pl.when(r < z)
-            def _():
-                s_ref[dest, k] = natural.astype(s_ref.dtype)
-
-            @pl.when(r > z)
-            def _():
-                s_ref[dest, k] = swap_rows(natural, size).astype(s_ref.dtype)
-
-            @pl.when(r == z)
-            def _():
-                s_ref[dest, k] = (natural - swap_rows(natural, size)).astype(s_ref.dtype)
+            start = dest * piece // 128 * 128
+            stop = min(start + width, staged.shape[1])
+            if stop - start < width:
+                s_ref[dest, k, :, pl.ds(width - 256, 256)] = jnp.zeros(
+                    (size * size, 256), s_ref.dtype)
+            s_ref[dest, k, :, pl.ds(0, stop - start)] = staged[:, start:stop]
 
     acc[...] = jnp.zeros_like(acc)
     fetch.wait()
@@ -142,8 +144,9 @@
             g[z, m] = jnp.concatenate([first, second], axis=0).astype(g.dtype)
         else:
             tail = first[:, half_width:]
-            fill = jnp.zeros((half, 2 * half_width - width), jnp.float32)
-            tail = jnp.concatenate([tail, fill], axis=1)
+            if 2 * half_width > width:
+                fill = jnp.zeros((half, 2 * half_width - width), jnp.float32)
+                tail = jnp.concatenate([tail, fill], axis=1)
             g[z, m, :, pl.ds(0, half_width)] = jnp.concatenate(
                 [first[:, :half_width], tail], axis=0).astype(g.dtype)
 
@@ -245,8 +248,11 @@
                         [one, two], axis=0).astype(dd.dtype)
 
         pltpu.make_async_copy(v_hbm.at[k], v.at[k], lv.at[k]).wait()
+        wide = dd[...].reshape(acc.shape[1], width).astype(f32)
+        shift = lax.rem(width - lax.rem(r * piece, 128), width)
+        aligned = pltpu.roll(wide, shift, 1)[:, :piece].astype(dd.dtype)
         acc[...] += lax.dot_general(
-            v[k], dd[...].reshape(acc.shape[1], dd.shape[2]),
+            v[k], aligned,
             (((1,), (1,)), ((), ())), preferred_element_type=f32)
 
     last = lax.max(z, n - 1 - z)
@@ -352,19 +358,13 @@
                        q_recv.at[s, source], row=source).wait_recv()
                 total += rowrecv[s, source].astype(jnp.float32)
 
-            first, second, other, _swapped = blocks_of(s)
-
-            @pl.when(number_of(s) < off_pairs)
-            def _():
-                kept = masked(total, first, second)
-                res[s, 0] = kept.astype(res.dtype)
-                res[s, 1] = (-swap_rows(kept, size)).astype(res.dtype)
-
-            @pl.when(number_of(s) >= off_pairs)
-            def _():
-                res[s, 0] = masked(unpack_rows(total[:half], size), first, first).astype(res.dtype)
-                res[s, 1] = masked(unpack_rows(total[half:], size), other, other).astype(res.dtype)
-
+            first, second, other, swapped = blocks_of(s)
+            apart = number_of(s) < off_pairs
+            rounded = total.astype(res.dtype)
+            one = reorder(jnp.where(apart, same, packed_first), rounded)
+            two = reorder(jnp.where(apart, -swapped_rows, packed_second), rounded)
+            res[s, 0] = masked(one, first, second).astype(res.dtype)
+            res[s, 1] = masked(two, swapped, other).astype(res.dtype)
             deliver(s, "start")
 
     for source in range(n):
@@ -414,7 +414,8 @@
 
 def ladder_blocks(amplitudes, integrals, occ_offsets, slab, n, reps):
     size, kb, _, pairs = amplitudes.shape
-    rows, width = size * size, pairs // n
+    rows, piece = size * size, pairs // n
+    width = max(-(-(t * piece % 128 + piece) // 128) * 128 for t in range(n))
     slab_rows = integrals.shape[1]
     numbers = n * (n - 1) // 2 + -(-n // 2)
     chunks = -(-kb // 2)
@@ -438,7 +439,7 @@
             pltpu.VMEM((kb, n, n, rows, width), bf16),
             pltpu.VMEM((n, chunks, rows, width), bf16),
             pltpu.VMEM((reps * per_rep, rows, width), bf16),
-            pltpu.VMEM((kb, slab_rows, width), bf16),
+            pltpu.VMEM((kb, slab_rows, piece), bf16),
             pltpu.VMEM((slab_rows, reps * per_rep * rows), jnp.float32),
             pltpu.VMEM((reps, per_rep, rows, slab_rows), bf16),
             pltpu.VMEM((max(reps - 1, 1), per_rep, rows, slab_rows), bf16),

time: 54.9 us -> 55.1 us (level)
  no operation moved by 1% of the time
where the time goes in v6:
time: 55.1 us; the launch traced here: 54.9 us
  Pallas kernels  53.3 us (97%)
  other arithmetic  1.66 us (3%)
    pallas_call x1, Pallas kernels, ladder_blocks(): pl.pallas_call(functools.partial(kernel, n, reps, size), out_shape=jax.Sh...  53.3 us
    neg x1, other arithmetic, shards(): -ladder_blocks(jnp.transpose(amplitudes, (0, 2, 1, 3)), jnp.transpose(int...  1.66 us

profile of v6, /device:TPU:1, one launch (start us, length us, event | category | flops | bytes accessed | tf_op | source)
XLA Modules:
  0.0 54.9 jit_solution(15792353229275482562)
XLA Ops:
  0.0 53.3 %ladder_blocks.1 = bf16[4,4,5184]{2,1,0:T(4,128)(2,1)} custom-call(bf16[4,3,4,5184]{3,2,1,0:T(4,128)(2,1)} %bitcast.3, bf16[3,1296,1296]{2,1,0:T(8,128)(2,1)} %bitcast.2, s32[9]{0:T(128)} %occ_ref.1, s32[2]{0:T(128)} %slab_ref.1), custom_call_target="tpu_custom_call" | custom-call | tf_op jit(solution)/shard_map/ladder_blocks/pallas_call | solution.py:425
  53.3 1.7 %neg.3 = bf16[4,4,5184]{2,1,0:T(4,128)(2,1)} negate(bf16[4,4,5184]{2,1,0:T(4,128)(2,1)} %ladder_blocks.1) | non-fusion elementwise | flops 82944 | bytes 331776 | tf_op jit(solution)/shard_map/neg | solution.py:473

commit v7 on v6

--- a/solution.py
+++ b/solution.py
@@ -65,20 +65,27 @@
 
     fetch = pltpu.make_async_copy(a_hbm, a_ref, la)
     fetch.start()
-    for k in range(kb):
-        pltpu.make_async_copy(v_hbm.at[k], v.at[k], lv.at[k]).start()
 
     barrier = pltpu.get_barrier_semaphore()
-    devices = n * n * reps
-    me = (r * n + z) * reps + p
-
-    @pl.loop(1, devices)
-    def _(off):
-        other = lax.rem(me + off, devices)
+
+    def greet(**where):
+        target = {"row": r, "col": z, "rep": p, **where}
         pl.semaphore_signal(
-            barrier, inc=1,
-            device_id=(other // (n * reps), lax.rem(other // reps, n), lax.rem(other, reps)),
+            barrier, inc=1, device_id=(target["row"], target["col"], target["rep"]),
             device_id_type=MESH)
+
+    for off in range(1, n):
+        greet(row=lax.rem(r + off, n))
+    for off in range(1, reps):
+        greet(rep=lax.rem(p + off, reps))
+
+    @pl.when(z > 0)
+    def _():
+        greet(col=lax.max(z - 1, 0))
+
+    @pl.when(z < n - 1)
+    def _():
+        greet(col=lax.min(z + 1, n - 1))
 
     def shuffle(k, off):
         dest = lax.rem(r + off, n)
@@ -107,7 +114,8 @@
     stage(0)
     if reps * per_rep != numbers:
         dd[...] = jnp.zeros_like(dd)
-    pl.semaphore_wait(barrier, devices - 1)
+    beside = (z > 0).astype(jnp.int32) + (z < n - 1).astype(jnp.int32)
+    pl.semaphore_wait(barrier, n - 1 + reps - 1 + beside)
     def send_shuffle(k):
         for off in range(1, n):
             shuffle(k, off).start()
@@ -168,6 +176,7 @@
                     to_left(k, c).start()
                 if c < n - 1:
                     to_right(k, c).start()
+        pltpu.make_async_copy(v_hbm.at[k], v.at[k], lv.at[k]).start()
         if k + 2 < kb:
             stage(k + 2)
             send_shuffle(k + 2)

time: 55.1 us -> 52 us (0.944)
  Pallas kernels: 53.3 us -> 50.1 us
    pallas_call x1, Pallas kernels: 53.3 us -> 50.1 us  [ladder_blocks(): pl.pallas_call(functools.partial(kernel, n, reps, size), out_shape=jax.Sh...]
where the time goes in v7:
time: 52 us; the launch traced here: 51.8 us
  Pallas kernels  50.1 us (96%)
  other arithmetic  1.66 us (3%)
    pallas_call x1, Pallas kernels, ladder_blocks(): pl.pallas_call(functools.partial(kernel, n, reps, size), out_shape=jax.Sh...  50.1 us
    neg x1, other arithmetic, shards(): -ladder_blocks(jnp.transpose(amplitudes, (0, 2, 1, 3)), jnp.transpose(int...  1.66 us

profile of v7, /device:TPU:1, one launch (start us, length us, event | category | flops | bytes accessed | tf_op | source)
XLA Modules:
  0.0 51.8 jit_solution(1953654467923615472)
XLA Ops:
  0.0 50.1 %ladder_blocks.1 = bf16[4,4,5184]{2,1,0:T(4,128)(2,1)} custom-call(bf16[4,3,4,5184]{3,2,1,0:T(4,128)(2,1)} %bitcast.3, bf16[3,1296,1296]{2,1,0:T(8,128)(2,1)} %bitcast.2, s32[9]{0:T(128)} %occ_ref.1, s32[2]{0:T(128)} %slab_ref.1), custom_call_target="tpu_custom_call" | custom-call | tf_op jit(solution)/shard_map/ladder_blocks/pallas_call | solution.py:434
  50.2 1.7 %neg.3 = bf16[4,4,5184]{2,1,0:T(4,128)(2,1)} negate(bf16[4,4,5184]{2,1,0:T(4,128)(2,1)} %ladder_blocks.1) | non-fusion elementwise | flops 82944 | bytes 331776 | tf_op jit(solution)/shard_map/neg | solution.py:482

commit v8 on v7

--- a/solution.py
+++ b/solution.py
@@ -257,11 +257,11 @@
                         [one, two], axis=0).astype(dd.dtype)
 
         pltpu.make_async_copy(v_hbm.at[k], v.at[k], lv.at[k]).wait()
-        wide = dd[...].reshape(acc.shape[1], width).astype(f32)
+        wide = dd[...].reshape(acc.shape[0], width).astype(f32)
         shift = lax.rem(width - lax.rem(r * piece, 128), width)
         aligned = pltpu.roll(wide, shift, 1)[:, :piece].astype(dd.dtype)
         acc[...] += lax.dot_general(
-            v[k], aligned,
+            aligned, v[k],
             (((1,), (1,)), ((), ())), preferred_element_type=f32)
 
     last = lax.max(z, n - 1 - z)
@@ -274,7 +274,7 @@
                 def _():
                     multiply(k)
 
-    pb[...] = acc[...].T.reshape(pb.shape).astype(pb.dtype)
+    pb[...] = acc[...].reshape(pb.shape).astype(pb.dtype)
 
     def swap_reps(off):
         other = lax.rem(p + off, reps)
@@ -449,7 +449,7 @@
             pltpu.VMEM((n, chunks, rows, width), bf16),
             pltpu.VMEM((reps * per_rep, rows, width), bf16),
             pltpu.VMEM((kb, slab_rows, piece), bf16),
-            pltpu.VMEM((slab_rows, reps * per_rep * rows), jnp.float32),
+            pltpu.VMEM((reps * per_rep * rows, slab_rows), jnp.float32),
             pltpu.VMEM((reps, per_rep, rows, slab_rows), bf16),
             pltpu.VMEM((max(reps - 1, 1), per_rep, rows, slab_rows), bf16),
             pltpu.VMEM((per_rep, rows, slab_rows), bf16),

time: 52 us -> 51.9 us (level)
  no operation moved by 1% of the time
where the time goes in v8:
time: 51.9 us; the launch traced here: 51.7 us
  Pallas kernels  50 us (96%)
  other arithmetic  1.66 us (3%)
    pallas_call x1, Pallas kernels, ladder_blocks(): pl.pallas_call(functools.partial(kernel, n, reps, size), out_shape=jax.Sh...  50 us
    neg x1, other arithmetic, shards(): -ladder_blocks(jnp.transpose(amplitudes, (0, 2, 1, 3)), jnp.transpose(int...  1.66 us

profile of v8, /device:TPU:1, one launch (start us, length us, event | category | flops | bytes accessed | tf_op | source)
XLA Modules:
  0.0 51.7 jit_solution(1931112600710676137)
XLA Ops:
  0.0 50.0 %ladder_blocks.1 = bf16[4,4,5184]{2,1,0:T(4,128)(2,1)} custom-call(bf16[4,3,4,5184]{3,2,1,0:T(4,128)(2,1)} %bitcast.3, bf16[3,1296,1296]{2,1,0:T(8,128)(2,1)} %bitcast.2, s32[9]{0:T(128)} %occ_ref.1, s32[2]{0:T(128)} %slab_ref.1), custom_call_target="tpu_custom_call" | custom-call | tf_op jit(solution)/shard_map/ladder_blocks/pallas_call | solution.py:434
  50.0 1.7 %neg.3 = bf16[4,4,5184]{2,1,0:T(4,128)(2,1)} negate(bf16[4,4,5184]{2,1,0:T(4,128)(2,1)} %ladder_blocks.1) | non-fusion elementwise | flops 82944 | bytes 331776 | tf_op jit(solution)/shard_map/neg | solution.py:482
